TPU v7x, 32 devices: a whole 2x2x4 slice. The times are simulated.
32 devices in a mesh: wide: 8 (over y, x, core), rep: 4 (over z).
Axes of the slice: x: 2, y: 2, z: 4, core: 2. Of those that a mesh axis runs over, the one named last changes fastest.
Arguments:
- passages: bfloat16 [32768, 1024], P(('wide', 'rep')), may hold values from -6 to 6
- cluster_ids: int32 [32768], P(('wide', 'rep')), may hold values from 0 to 131071, as said below
- w_first: bfloat16 [1024, 1024], replicated, may hold values from -0.1875 to 0.1875
- w_second: bfloat16 [1024, 256], replicated, may hold values from -0.1875 to 0.1875
- centroids: bfloat16 [131072, 256], P('wide'), may hold values from -6 to 6
Outputs:
- refreshed: bfloat16 [131072, 256], P(('wide', 'rep'))
- residuals: bfloat16 [32768, 256], P(('wide', 'rep'))
Inputs may be any that keep to these rules, and one draw needn't show every extreme that they name: The owner of a passage is cluster_ids // 16384. Among the 1024 rows of one device (aligned blocks), at most 384 have any one owner; in every draw one owner gets exactly 384 rows from every device's block.
All inputs are finite; a program needn't handle non-finite values.
Results may differ from a plain program's by a relative error of at most 0.015.
Values may be sent and summed in bfloat16 or wider, within the bound.
A program may use at most 128 MiB of HBM per device.

v0:
```python
import jax
import jax.numpy as jnp
from jax import lax
from jax.sharding import PartitionSpec as P


def refresh(current, summed):
    updated = current.astype(jnp.float32) + summed
    return (
        updated * lax.rsqrt(jnp.mean(updated * updated, axis=-1, keepdims=True) + 1e-06)
    ).astype(jnp.bfloat16)


def body(passages, cluster_ids, w_first, w_second, centroids):
    tok_rows = passages.shape[0]
    owners = lax.axis_size("wide")
    cent_rows = centroids.shape[0]
    emb_width = w_second.shape[1]
    capacity = 3 * tok_rows // owners
    hidden = jax.nn.gelu(
        jnp.dot(passages, w_first, preferred_element_type=jnp.float32), approximate=True
    ).astype(jnp.bfloat16)
    projected = jnp.dot(hidden, w_second, preferred_element_type=jnp.float32)
    embedded = (
        projected * lax.rsqrt(jnp.mean(projected * projected, axis=-1, keepdims=True) + 1e-06)
    ).astype(jnp.bfloat16)
    owner_of = cluster_ids // cent_rows
    local_id = cluster_ids - owner_of * cent_rows
    member = (owner_of[:, None] == jnp.arange(owners, dtype=jnp.int32)[None, :]).astype(jnp.int32)
    before = jnp.cumsum(member, axis=0) - member
    slot_of = jnp.sum(before * member, axis=1)
    target = owner_of * capacity + slot_of
    counts = jnp.sum(member, axis=0)
    starts = jnp.cumsum(counts) - counts
    order = jnp.argsort(owner_of, stable=True)
    slot_index = jnp.arange(capacity, dtype=jnp.int32)[None, :]
    valid = (slot_index < counts[:, None]).reshape(owners * capacity)
    position = jnp.minimum(starts[:, None] + slot_index, tok_rows - 1).reshape(owners * capacity)
    source = order[position]
    outgoing = jnp.where(valid[:, None], embedded[source], jnp.zeros((), jnp.bfloat16))
    out_ids = jnp.where(valid, local_id[source], -1)
    incoming, in_ids = (
        lax.all_to_all(outgoing, "wide", split_axis=0, concat_axis=0, tiled=True),
        lax.all_to_all(out_ids, "wide", split_axis=0, concat_axis=0, tiled=True),
    )
    block_rows = min(cent_rows, 2048)
    block_count = cent_rows // block_rows

    def one_block(block_start):
        row_ids = block_start + jnp.arange(block_rows, dtype=jnp.int32)
        selector = (row_ids[:, None] == in_ids[None, :]).astype(jnp.bfloat16)
        return jnp.dot(selector, incoming, preferred_element_type=jnp.float32)

    block_starts = jnp.arange(block_count, dtype=jnp.int32) * block_rows
    partial_value = lax.map(one_block, block_starts).reshape(cent_rows, emb_width)
    safe_ids = jnp.where(in_ids >= 0, in_ids, 0)
    replicas = lax.axis_size("rep")
    share_rows = cent_rows // replicas
    first_row = lax.axis_index("rep") * share_rows
    summed = lax.psum(partial_value.astype(jnp.bfloat16), "rep").astype(jnp.float32)
    fresh_table = refresh(centroids, summed)
    own_rows = lax.dynamic_slice_in_dim(fresh_table, first_row, share_rows, 0)
    picked = fresh_table[safe_ids]
    returned = lax.all_to_all(picked, "wide", split_axis=0, concat_axis=0, tiled=True)
    gathered_rows = returned[target]
    residuals = (embedded.astype(jnp.float32) - gathered_rows.astype(jnp.float32)).astype(
        jnp.bfloat16
    )
    return (own_rows, residuals)


def solution(mesh):
    return jax.shard_map(
        body,
        mesh=mesh,
        in_specs=(P(("wide", "rep"), None), P(("wide", "rep")), P(), P(), P("wide", None)),
        out_specs=(P(("wide", "rep"), None), P(("wide", "rep"), None)),
        check_vma=False,
    )
```

profile of v0, /device:TPU:4, one launch (start us, length us, event | category | flops | bytes accessed | tf_op | source)
XLA Modules:
  0.0 522.1 jit_solution(14302943597052908508)
XLA Ops:
  8.0 2.3 reduce-window.19
  11.3 4.4 sort.17
  15.7 12.6 %gather_fusion = s32[3072]{0:T(1024)S(1)} fusion(s32[1024]{0:T(1024)S(1)} %get-tuple-element.30, s32[3072]{0:T(1024)S(1)} %broadcast_clamp_fusion.1), kind=kCustom, calls=%fused_computation | custom fusion | bytes 36864 | tf_op jit(solution)/shard_map/gather | solution.py:39
  28.4 12.6 %gather_fusion.1 = s32[3072]{0:T(1024)S(1)} fusion(s32[1024]{0:T(1024)S(1)} %get-tuple-element.51, s32[3072]{0:T(1024)S(1)} %broadcast_clamp_fusion.2), kind=kCustom, calls=%fused_computation.1 | custom fusion | bytes 36864 | tf_op jit(solution)/shard_map/gather | solution.py:41
  41.7 4.2 all-to-all-start
  46.0 5.0 multiply_reduce_fusion.1
  51.0 1.0 copy-done.2
  52.9 1.2 copy.14
  54.1 13.0 %gather_fusion.2 = bf16[3072,256]{1,0:T(8,128)(2,1)} fusion(bf16[1024,256]{1,0:T(8,128)(2,1)S(1)} %copy.14, s32[3072]{0:T(1024)S(1)} %broadcast_clamp_fusion.2), kind=kCustom, calls=%fused_computation.2 | custom fusion | bytes 3158016 | tf_op jit(solution)/shard_map/gather | solution.py:40
  67.2 2.7 broadcast_select_fusion
  69.9 4.2 all-to-all-start.1
  74.4 19.4 %all-to-all-done.1 = bf16[8,384,256]{2,1,0:T(8,128)(2,1)} async-done(((bf16[8,384,256]{2,1,0:T(8,128)(2,1)}), bf16[8,384,256]{2,1,0:T(8,128)(2,1)}, u32[]{:S(2)}, u32[]{:S(2)}) %all-to-all-start.1) | async-done | bytes 1572896 | tf_op jit(solution)/shard_map/all_to_all | solution.py:43
  93.7 60.6 %while.10 = (s32[]{:T(128)}, bf16[8,2048,256]{2,1,0:T(8,128)(2,1)}, s32[8]{0:T(128)S(1)}, s32[3072]{0:T(1024)S(1)}, bf16[3072,256]{1,0:T(8,128)(2,1)}, /*index=5*/s32[]{:T(128)}) while((s32[]{:T(128)}, bf16[8,2048,256]{2,1,0:T(8,128)(2,1)}, s32[8]{0:T(128)S(1)}, s32[3072]{0:T(1024)S(1)}, bf16[3072,256]{1,0:T(8,128)(2,1)}, ...), condition=%wide.region_5.6_spmd, body=%wide.region_4.5_spmd.sunk | while | flops 3227518976 | bytes 3699285 | solution.py:55
  95.0 6.4 %fusion.43 = bf16[8,2048,256]{2,1,0:T(8,128)(2,1)} fusion(bf16[8,2048,256]{2,1,0:T(8,128)(2,1)} %get-tuple-element.94, s32[]{:T(128)} %get-tuple-element.93, bf16[3072,256]{1,0:T(8,128)(2,1)} %get-tuple-element.103, s32[3072]{0:T(1024)S(1)} %get-tuple-element.102, s32[2048]{0:T(1024)S(1)} %iota_add_fusion.2), kind=kOutput, calls=%fused_computation.10.clone.1 | convolution fusion | flops 3227516928 | bytes 3691008 | tf_op jit(solution)/shard_map/while/body/eval_jaxpr/dot_general | solution.py:52
  102.6 6.3 %fusion.43 = bf16[8,2048,256]{2,1,0:T(8,128)(2,1)} fusion(bf16[8,2048,256]{2,1,0:T(8,128)(2,1)} %get-tuple-element.94, s32[]{:T(128)} %get-tuple-element.93, bf16[3072,256]{1,0:T(8,128)(2,1)} %get-tuple-element.103, s32[3072]{0:T(1024)S(1)} %get-tuple-element.102, s32[2048]{0:T(1024)S(1)} %iota_add_fusion.2), kind=kOutput, calls=%fused_computation.10.clone.1 | convolution fusion | flops 3227516928 | bytes 3691008 | tf_op jit(solution)/shard_map/while/body/eval_jaxpr/dot_general | solution.py:52
  110.1 6.3 %fusion.43 = bf16[8,2048,256]{2,1,0:T(8,128)(2,1)} fusion(bf16[8,2048,256]{2,1,0:T(8,128)(2,1)} %get-tuple-element.94, s32[]{:T(128)} %get-tuple-element.93, bf16[3072,256]{1,0:T(8,128)(2,1)} %get-tuple-element.103, s32[3072]{0:T(1024)S(1)} %get-tuple-element.102, s32[2048]{0:T(1024)S(1)} %iota_add_fusion.2), kind=kOutput, calls=%fused_computation.10.clone.1 | convolution fusion | flops 3227516928 | bytes 3691008 | tf_op jit(solution)/shard_map/while/body/eval_jaxpr/dot_general | solution.py:52
  117.7 6.3 %fusion.43 = bf16[8,2048,256]{2,1,0:T(8,128)(2,1)} fusion(bf16[8,2048,256]{2,1,0:T(8,128)(2,1)} %get-tuple-element.94, s32[]{:T(128)} %get-tuple-element.93, bf16[3072,256]{1,0:T(8,128)(2,1)} %get-tuple-element.103, s32[3072]{0:T(1024)S(1)} %get-tuple-element.102, s32[2048]{0:T(1024)S(1)} %iota_add_fusion.2), kind=kOutput, calls=%fused_computation.10.clone.1 | convolution fusion | flops 3227516928 | bytes 3691008 | tf_op jit(solution)/shard_map/while/body/eval_jaxpr/dot_general | solution.py:52
  125.2 6.4 %fusion.43 = bf16[8,2048,256]{2,1,0:T(8,128)(2,1)} fusion(bf16[8,2048,256]{2,1,0:T(8,128)(2,1)} %get-tuple-element.94, s32[]{:T(128)} %get-tuple-element.93, bf16[3072,256]{1,0:T(8,128)(2,1)} %get-tuple-element.103, s32[3072]{0:T(1024)S(1)} %get-tuple-element.102, s32[2048]{0:T(1024)S(1)} %iota_add_fusion.2), kind=kOutput, calls=%fused_computation.10.clone.1 | convolution fusion | flops 3227516928 | bytes 3691008 | tf_op jit(solution)/shard_map/while/body/eval_jaxpr/dot_general | solution.py:52
  132.9 6.3 %fusion.43 = bf16[8,2048,256]{2,1,0:T(8,128)(2,1)} fusion(bf16[8,2048,256]{2,1,0:T(8,128)(2,1)} %get-tuple-element.94, s32[]{:T(128)} %get-tuple-element.93, bf16[3072,256]{1,0:T(8,128)(2,1)} %get-tuple-element.103, s32[3072]{0:T(1024)S(1)} %get-tuple-element.102, s32[2048]{0:T(1024)S(1)} %iota_add_fusion.2), kind=kOutput, calls=%fused_computation.10.clone.1 | convolution fusion | flops 3227516928 | bytes 3691008 | tf_op jit(solution)/shard_map/while/body/eval_jaxpr/dot_general | solution.py:52
  140.4 6.3 %fusion.43 = bf16[8,2048,256]{2,1,0:T(8,128)(2,1)} fusion(bf16[8,2048,256]{2,1,0:T(8,128)(2,1)} %get-tuple-element.94, s32[]{:T(128)} %get-tuple-element.93, bf16[3072,256]{1,0:T(8,128)(2,1)} %get-tuple-element.103, s32[3072]{0:T(1024)S(1)} %get-tuple-element.102, s32[2048]{0:T(1024)S(1)} %iota_add_fusion.2), kind=kOutput, calls=%fused_computation.10.clone.1 | convolution fusion | flops 3227516928 | bytes 3691008 | tf_op jit(solution)/shard_map/while/body/eval_jaxpr/dot_general | solution.py:52
  147.9 6.3 %fusion.43 = bf16[8,2048,256]{2,1,0:T(8,128)(2,1)} fusion(bf16[8,2048,256]{2,1,0:T(8,128)(2,1)} %get-tuple-element.94, s32[]{:T(128)} %get-tuple-element.93, bf16[3072,256]{1,0:T(8,128)(2,1)} %get-tuple-element.103, s32[3072]{0:T(1024)S(1)} %get-tuple-element.102, s32[2048]{0:T(1024)S(1)} %iota_add_fusion.2), kind=kOutput, calls=%fused_computation.10.clone.1 | convolution fusion | flops 3227516928 | bytes 3691008 | tf_op jit(solution)/shard_map/while/body/eval_jaxpr/dot_general | solution.py:52
  154.3 291.3 %all-reduce.2.cloned.1.call-done = bf16[16384,256]{1,0:T(8,128)(2,1)} async-done(((bf16[16384,256]{1,0:T(8,128)(2,1)}), bf16[16384,256]{1,0:T(8,128)(2,1)}) %all-reduce.2.cloned.1.call-update) | async-done | bytes 8388624 | tf_op jit(solution)/shard_map/psum | solution.py:60
  445.7 7.6 %multiply_reduce_fusion = f32[16384]{0:T(1024)S(1)} fusion(bf16[16384,256]{1,0:T(8,128)(2,1)} %all-reduce.2.cloned.1.call-done, bf16[16384,256]{1,0:T(8,128)(2,1)} %param.11), kind=kLoop, calls=%fused_computation.13 | loop fusion | flops 20955136 | bytes 16842752 | tf_op jit(solution)/shard_map/reduce_sum | solution.py:10
  453.9 8.1 %multiply_convert_fusion = bf16[16384,256]{1,0:T(8,128)(2,1)} fusion(bf16[16384,256]{1,0:T(8,128)(2,1)S(1)} %copy-done.1, bf16[16384,256]{1,0:T(8,128)(2,1)} %param.11, f32[16384]{0:T(1024)S(1)} %add_rsqrt_fusion), kind=kLoop, calls=%fused_computation.12 | loop fusion | flops 20971520 | bytes 25231360 | tf_op jit(solution)/shard_map/convert_element_type | solution.py:11
  462.0 16.6 %gather_fusion.3 = bf16[3072,256]{1,0:T(8,128)(2,1)} fusion(bf16[16384,256]{1,0:T(8,128)(2,1)} %multiply_convert_fusion, s32[3072]{0:T(1024)S(1)} %broadcast_clamp_fusion), kind=kCustom, calls=%fused_computation.3 | custom fusion | bytes 3158016 | tf_op jit(solution)/shard_map/gather | solution.py:63
  478.6 4.7 all-to-all-start.2
  483.3 3.1 constant_dynamic-slice_fusion
  486.4 16.5 %all-to-all-done.2 = bf16[8,384,256]{2,1,0:T(8,128)(2,1)} async-done(((bf16[8,384,256]{2,1,0:T(8,128)(2,1)}), bf16[8,384,256]{2,1,0:T(8,128)(2,1)}, u32[]{:S(2)}, u32[]{:S(2)}) %all-to-all-start.2) | async-done | bytes 1572896 | tf_op jit(solution)/shard_map/all_to_all | solution.py:64
  502.9 6.2 %gather_fusion.4 = bf16[1024,256]{1,0:T(8,128)(2,1)} fusion(bf16[3072,256]{1,0:T(8,128)(2,1)} %bitcast.14, s32[1024]{0:T(1024)S(1)} %get-tuple-element.50), kind=kCustom, calls=%fused_computation.4 | custom fusion | bytes 1052672 | tf_op jit(solution)/shard_map/gather | solution.py:65
  509.2 2.0 copy.15
  511.2 2.0 subtract_convert_fusion
  513.2 2.0 copy.16
  (55 shorter events, 14.3 us)
Async XLA Ops:
  7.2 38.8 %copy-start = (bf16[1024,1024]{1,0:T(8,128)(2,1)S(1)}, bf16[1024,1024]{1,0:T(8,128)(2,1)}, u32[]{:S(2)}) copy-start(bf16[1024,1024]{1,0:T(8,128)(2,1)} %param.7) | copy-start | bytes 6291460
  15.7 12.7 %copy-start.4 = (s32[1024]{0:T(1024)S(1)}, s32[1024]{0:T(1024)}, u32[]{:S(2)}) copy-start(s32[1024]{0:T(1024)} %param.8) | copy-start | bytes 12292
  41.7 28.2 %all-to-all-start = ((s32[8,384,1]{1,2,0:T(1,128)}), s32[8,384,1]{1,2,0:T(1,128)S(1)}, u32[]{:S(2)}, u32[]{:S(2)}) async-start(s32[8,384,1]{1,2,0:T(1,128)} %copy.13), calls=%async_computation | async-start | bytes 24576 | tf_op jit(solution)/shard_map/all_to_all | solution.py:44
  51.0 1.0 copy-start.2
  69.9 23.9 %all-to-all-start.1 = ((bf16[8,384,256]{2,1,0:T(8,128)(2,1)}), bf16[8,384,256]{2,1,0:T(8,128)(2,1)}, u32[]{:S(2)}, u32[]{:S(2)}) async-start(bf16[8,384,256]{2,1,0:T(8,128)(2,1)} %broadcast_select_fusion), calls=%async_computation.1 | async-start | bytes 3145728 | tf_op jit(solution)/shard_map/all_to_all | solution.py:43
  74.1 371.5 %all-reduce.2.cloned.1.call-start = ((), (), s32[]{:S(2)}) async-start(), calls=%async_computation.3 | async-start | bytes 16777216 | tf_op jit(solution)/shard_map/psum | solution.py:60
  445.7 8.3 %copy-start.1 = (bf16[16384,256]{1,0:T(8,128)(2,1)S(1)}, bf16[16384,256]{1,0:T(8,128)(2,1)}, u32[]{:S(2)}) copy-start(bf16[16384,256]{1,0:T(8,128)(2,1)} %all-reduce.2.cloned.1.call-done) | copy-start | bytes 25165828
  478.6 24.4 %all-to-all-start.2 = ((bf16[8,384,256]{2,1,0:T(8,128)(2,1)}), bf16[8,384,256]{2,1,0:T(8,128)(2,1)}, u32[]{:S(2)}, u32[]{:S(2)}) async-start(bf16[8,384,256]{2,1,0:T(8,128)(2,1)} %bitcast.48), calls=%async_computation.2 | async-start | bytes 3145728 | tf_op jit(solution)/shard_map/all_to_all | solution.py:64
  483.3 27.9 %copy-start.3 = (f32[1024,256]{0,1:T(8,128)S(1)}, f32[1024,256]{0,1:T(8,128)}, u32[]{:S(2)}) copy-start(f32[1024,256]{0,1:T(8,128)} %copy-done.2) | copy-start | bytes 3145732
Sparse Core Ops, SparseCore 0:
  154.4 291.1 all-reduce.1
where the time goes:
time: 525 us; the launch traced here: 522 us
  waiting for transfers between devices  327 us (62%)
  local copies, waits for them, and re-layouts  76.7 us (15%)
  matrix products  55.6 us (11%)
  other arithmetic  34.8 us (7%)
  between operations  14.2 us (3%)
  starting transfers between devices  13.4 us (3%)
    psum x1, waiting for transfers between devices, body(): lax.psum(partial_value.astype(jnp.bfloat16), 'rep').astype(jnp.float32)  291 us
    dot_general x8, matrix products, one_block(): return jnp.dot(selector, incoming, preferred_element_type=jnp.float32)  50.7 us
    all_to_all x1, waiting for transfers between devices, body(): lax.all_to_all(outgoing, 'wide', split_axis=0, concat_axis=0, tiled=True)  19.4 us
    gather x1, local copies, waits for them, and re-layouts, body(): picked = fresh_table[safe_ids]  16.6 us
    all_to_all x1, waiting for transfers between devices, body(): lax.all_to_all(picked, 'wide', split_axis=0, concat_axis=0, tiled=True)  16.5 us
    gather x1, local copies, waits for them, and re-layouts, body(): embedded[source]  13 us
    gather x2, local copies, waits for them, and re-layouts, body(): out_ids = jnp.where(valid, local_id[source], -1)  12.6 us
    gather x1, local copies, waits for them, and re-layouts, body(): source = order[position]  12.6 us
  transfers between devices with their start and end apart: 4, of which 3 were waited for; matrix products, arithmetic and copies ran while one was open for 5% of the time, Pallas kernels for 0%

commit v1 on v0

v1 whole, which is shorter than its diff:
```python
import functools

import jax
import jax.numpy as jnp
from jax import lax
from jax.experimental import pallas as pl
from jax.experimental.pallas import tpu as pltpu
from jax.sharding import PartitionSpec as P

CHUNK = 128
GROUP = 8
EPS = 1e-06


def normalised(values):
    return values * lax.rsqrt(jnp.mean(values * values, axis=-1, keepdims=True) + EPS)


def sums_kernel(
    scalars, first, last, emb, ids, cent, own_ids, own_cent, own_emb, order,
    out_table, out_res, chunks, slots, acc, cent_buf, tile_res, sems, cent_sem,
    *, blocks, per_block, tile, row_block,
):
    n_chunks = blocks * per_block
    share = out_table.shape[0]
    tok = own_ids.shape[0]
    wide = GROUP * CHUNK

    cent_copy = pltpu.make_async_copy(
        cent.at[pl.ds(pl.multiple_of(scalars[1], 16), share)], cent_buf, cent_sem
    )
    cent_copy.start()

    def build(job):
        def block(k, count):
            begin = first[job * blocks + k]
            end = last[job * blocks + k]
            lo = begin // CHUNK
            hi = jnp.where(end > begin, (end + CHUNK - 1) // CHUNK, lo)

            def put(c, n):
                chunks[n] = k * per_block + c
                return n + 1

            return lax.fori_loop(lo, hi, put, count)

        count = lax.fori_loop(0, blocks, block, 0)
        for extra in range(GROUP):
            chunks[count + extra] = n_chunks
        return (count + GROUP - 1) // GROUP

    def copies(group, slot):
        made = []
        for j in range(GROUP):
            at = jnp.minimum(chunks[group * GROUP + j], n_chunks - 1)
            made.append(
                pltpu.make_async_copy(
                    emb.at[pl.ds(pl.multiple_of(at * CHUNK, CHUNK), CHUNK)],
                    slots.at[slot, pl.ds(j * CHUNK, CHUNK)],
                    sems.at[slot, j],
                )
            )
        return made

    def run(groups, step):
        @pl.when(groups > 0)
        def _():
            for copy in copies(0, 0):
                copy.start()

        def body(group, carry):
            slot = lax.rem(group, 2)

            @pl.when(group + 1 < groups)
            def _():
                for copy in copies(group + 1, 1 - slot):
                    copy.start()

            for copy in copies(group, slot):
                copy.wait()
            row = [ids[pl.ds(chunks[group * GROUP + j], 1), :] for j in range(GROUP)]
            step(jnp.concatenate(row, axis=1), slot)
            return carry

        lax.fori_loop(0, groups, body, 0)

    acc[...] = jnp.zeros_like(acc)
    groups = build(0)

    def table_step(id_row, slot):
        def rows(m, carry):
            at = pl.multiple_of(m * row_block, row_block)
            wanted = scalars[0] + at + lax.broadcasted_iota(jnp.int32, (row_block, wide), 0)
            pick = (wanted == id_row).astype(jnp.float32).astype(jnp.bfloat16)
            acc[pl.ds(at, row_block), :] += jnp.dot(
                pick, slots[slot], preferred_element_type=jnp.float32
            )
            return carry

        lax.fori_loop(0, share // row_block, rows, 0)

    run(groups, table_step)
    cent_copy.wait()

    def finish(m, carry):
        at = pl.ds(pl.multiple_of(m * row_block, row_block), row_block)
        updated = cent_buf[at, :].astype(jnp.float32) + acc[at, :]
        out_table[at, :] = normalised(updated).astype(jnp.bfloat16)
        return carry

    lax.fori_loop(0, share // row_block, finish, 0)

    def one_tile(i, carry):
        at = pl.ds(pl.multiple_of(i * tile, tile), tile)
        part = acc.at[pl.ds(0, tile)]
        part[...] = jnp.zeros((tile, acc.shape[1]), jnp.float32)
        groups = build(i + 1)

        def tile_step(id_row, slot):
            pick = (own_ids[at, :] == id_row).astype(jnp.float32).astype(jnp.bfloat16)
            part[...] += jnp.dot(pick, slots[slot], preferred_element_type=jnp.float32)

        run(groups, tile_step)
        fresh = normalised(own_cent[at, :].astype(jnp.float32) + part[...]).astype(jnp.bfloat16)
        tile_res[at, :] = (own_emb[at, :].astype(jnp.float32) - fresh.astype(jnp.float32)).astype(
            jnp.bfloat16
        )
        return carry

    lax.fori_loop(0, tok // tile, one_tile, 0)

    def unsort(i, carry):
        at = pl.multiple_of(i * tile, tile)
        wanted = at + lax.broadcasted_iota(jnp.int32, (tile, tok), 0)
        pick = (wanted == order[...]).astype(jnp.float32).astype(jnp.bfloat16)
        out_res[pl.ds(at, tile), :] = jnp.dot(
            pick, tile_res[...], preferred_element_type=jnp.float32
        ).astype(jnp.bfloat16)
        return carry

    lax.fori_loop(0, tok // tile, unsort, 0)


def body(passages, cluster_ids, w_first, w_second, centroids):
    tok = passages.shape[0]
    owners = lax.axis_size("wide")
    reps = lax.axis_size("rep")
    blocks = owners * reps
    cent_rows, emb_width = centroids.shape
    share = cent_rows // reps
    capacity = 3 * tok // owners
    per_block = tok // CHUNK
    tile = min(256, tok)
    tiles = tok // tile
    wide_at = lax.axis_index("wide")
    rep_at = lax.axis_index("rep")

    sorted_ids, order = lax.sort((cluster_ids, lax.iota(jnp.int32, tok)), num_keys=1)
    all_ids = lax.all_gather(sorted_ids, ("wide", "rep"), axis=0, tiled=False)

    hidden = jax.nn.gelu(
        jnp.dot(passages, w_first, preferred_element_type=jnp.float32), approximate=True
    ).astype(jnp.bfloat16)
    projected = jnp.dot(hidden, w_second, preferred_element_type=jnp.float32)
    embedded = normalised(projected).astype(jnp.bfloat16)
    to_sorted = (order[:, None] == jnp.arange(tok, dtype=jnp.int32)[None, :]).astype(jnp.bfloat16)
    own_emb = jnp.dot(to_sorted, embedded, preferred_element_type=jnp.float32).astype(jnp.bfloat16)
    all_emb = lax.all_gather(own_emb, ("wide", "rep"), axis=0, tiled=True)

    mine = lax.dynamic_index_in_dim(all_ids.reshape(owners, reps, tok), rep_at, 1, keepdims=False)
    owner_base = wide_at * cent_rows
    begin = jnp.sum((mine < owner_base).astype(jnp.int32), axis=1)
    padded = jnp.pad(mine, ((0, 0), (0, capacity)))
    asked = jnp.stack(
        [lax.dynamic_slice(padded[k], (begin[k],), (capacity,)) for k in range(owners)]
    )
    local = jnp.clip(asked - owner_base, 0, cent_rows - 1).reshape(owners * capacity)
    picked = centroids[local]
    returned = lax.all_to_all(picked, "wide", split_axis=0, concat_axis=0, tiled=True)
    owner_of = sorted_ids // cent_rows
    starts = jnp.sum(
        (sorted_ids[None, :] < jnp.arange(owners, dtype=jnp.int32)[:, None] * cent_rows).astype(
            jnp.int32
        ),
        axis=1,
    )
    member = (owner_of[:, None] == jnp.arange(owners, dtype=jnp.int32)[None, :]).astype(jnp.int32)
    place = owner_of * capacity + lax.iota(jnp.int32, tok) - jnp.sum(member * starts[None, :], axis=1)
    own_cent = returned[place]

    share_base = owner_base + rep_at * share
    lows = jnp.concatenate([share_base[None], sorted_ids[::tile]])
    highs = jnp.concatenate([share_base[None] + share, sorted_ids[tile - 1 :: tile] + 1])
    first = jnp.sum((all_ids[None] < lows[:, None, None]).astype(jnp.int32), axis=2).reshape(-1)
    last = jnp.sum((all_ids[None] < highs[:, None, None]).astype(jnp.int32), axis=2).reshape(-1)
    scalars = jnp.stack([share_base, rep_at * share])
    id_rows = jnp.concatenate(
        [all_ids.reshape(blocks * per_block, CHUNK), jnp.full((8, CHUNK), -1, jnp.int32)]
    )

    smem = pl.BlockSpec(memory_space=pltpu.SMEM)
    vmem = pl.BlockSpec(memory_space=pltpu.VMEM)
    hbm = pl.BlockSpec(memory_space=pl.ANY)
    return pl.pallas_call(
        functools.partial(
            sums_kernel, blocks=blocks, per_block=per_block, tile=tile, row_block=min(512, share)
        ),
        out_shape=(
            jax.ShapeDtypeStruct((share, emb_width), jnp.bfloat16),
            jax.ShapeDtypeStruct((tok, emb_width), jnp.bfloat16),
        ),
        in_specs=[smem, smem, smem, hbm, vmem, hbm, vmem, vmem, vmem, vmem],
        out_specs=(vmem, vmem),
        scratch_shapes=[
            pltpu.SMEM((blocks * per_block + GROUP,), jnp.int32),
            pltpu.VMEM((2, GROUP * CHUNK, emb_width), jnp.bfloat16),
            pltpu.VMEM((share, emb_width), jnp.float32),
            pltpu.VMEM((share, emb_width), jnp.bfloat16),
            pltpu.VMEM((tok, emb_width), jnp.bfloat16),
            pltpu.SemaphoreType.DMA((2, GROUP)),
            pltpu.SemaphoreType.DMA,
        ],
        compiler_params=pltpu.CompilerParams(vmem_limit_bytes=48 * 1024 * 1024),
        cost_estimate=pl.CostEstimate(
            flops=30_000_000_000, bytes_accessed=40_000_000, transcendentals=0
        ),
    )(
        scalars, first, last, all_emb, id_rows, centroids, sorted_ids[:, None], own_cent, own_emb,
        order[None, :],
    )


def solution(mesh):
    return jax.shard_map(
        body,
        mesh=mesh,
        in_specs=(P(("wide", "rep"), None), P(("wide", "rep")), P(), P(), P("wide", None)),
        out_specs=(P(("wide", "rep"), None), P(("wide", "rep"), None)),
        check_vma=False,
    )
```

time: 525 us -> 240 us (0.46)
  waiting for transfers between devices: 327 us -> 18.2 us
  Pallas kernels: 0 us -> 75.4 us
  blocking collectives: 0 us -> 69.7 us
  local copies, waits for them, and re-layouts: 76.7 us -> 27.2 us
  matrix products: 55.6 us -> 6.65 us
  other arithmetic: 34.8 us -> 4.71 us
  between operations: 14.2 us -> 29.4 us
  starting transfers between devices: 13.4 us -> 5.9 us
    psum x1 -> x0, waiting for transfers between devices: 291 us -> none  [body(): lax.psum(partial_value.astype(jnp.bfloat16), 'rep').astype(jnp.float32)]
    pallas_call x0 -> x1, Pallas kernels: none -> 75.4 us  [body(): pl.pallas_call(functools.partial(sums_kernel, blocks=blocks, per_block=pe...]
    all_gather x0 -> x1, blocking collectives: none -> 69.7 us  [body(): all_ids = lax.all_gather(sorted_ids, ('wide', 'rep'), axis=0, tiled=False)]
    dot_general x8 -> x1, matrix products: 50.7 us -> 1.67 us  [body(): jnp.dot(to_sorted, embedded, preferred_element_type=jnp.float32)]
    gather x7 -> x2, local copies, waits for them, and re-layouts: 63.1 us -> 22.9 us  [the longest x1 16.7 us: body(): picked = centroids[local]]
    all_to_all x2 -> x0, waiting for transfers between devices: 19.4 us -> none  [the longest x1 19.4 us: body(): lax.all_to_all(outgoing, 'wide', split_axis=0, concat_axis=0, tiled=True)]
    convert_element_type x4 -> x0, other arithmetic: 11 us -> none  [the longest x1 8.06 us: refresh(): return (updated * lax.rsqrt(jnp.mean(updated * updated, axis=-1, keepdims...]
    all_to_all x2 -> x0, starting transfers between devices: 8.47 us -> none  [the longest x1 4.25 us: body(): lax.all_to_all(outgoing, 'wide', split_axis=0, concat_axis=0, tiled=True)]
  transfers between devices with their start and end apart: 4 -> 2, of which waited for: 3 -> 1; matrix products, arithmetic and copies ran while one was open for 5% -> 11% of each run, Pallas kernels for 0% -> 0%
where the time goes in v1:
time: 240 us; the launch traced here: 237 us
  Pallas kernels  75.4 us (31%)
  blocking collectives  69.7 us (29%)
  between operations  29.4 us (12%)
  local copies, waits for them, and re-layouts  27.2 us (11%)
  waiting for transfers between devices  18.2 us (8%)
  matrix products  6.65 us (3%)
  starting transfers between devices  5.9 us (2%)
  other arithmetic  4.71 us (2%)
    pallas_call x1, Pallas kernels, body(): pl.pallas_call(functools.partial(sums_kernel, blocks=blocks, per_block=pe...  75.4 us
    all_gather x1, blocking collectives, body(): all_ids = lax.all_gather(sorted_ids, ('wide', 'rep'), axis=0, tiled=False)  69.7 us
    all_to_all x1, waiting for transfers between devices, body(): lax.all_to_all(picked, 'wide', split_axis=0, concat_axis=0, tiled=True)  18.2 us
    gather x1, local copies, waits for them, and re-layouts, body(): picked = centroids[local]  16.7 us
    gather x1, local copies, waits for them, and re-layouts, body(): own_cent = returned[place]  6.22 us
    all_to_all x1, starting transfers between devices, body(): lax.all_to_all(picked, 'wide', split_axis=0, concat_axis=0, tiled=True)  5.87 us
    dot_general x1, matrix products, body(): projected = jnp.dot(hidden, w_second, preferred_element_type=jnp.float32)  4.98 us
  transfers between devices with their start and end apart: 2, of which 1 were waited for; matrix products, arithmetic and copies ran while one was open for 11% of the time, Pallas kernels for 0%

profile of v1, /device:TPU:4, one launch (start us, length us, event | category | flops | bytes accessed | tf_op | source)
XLA Modules:
  0.0 237.2 jit_solution(7107719485343144046)
XLA Ops:
  7.2 0.0 copy-start
  7.2 0.0 copy-start.3
  7.2 0.0 all-gather.3.cloned.1.call-start
  7.2 1.5 copy-done
  8.8 5.0 %multiply_reduce_fusion = (f32[1024]{0:T(1024)S(1)}, f32[1024,256]{0,1:T(8,128)S(1)}) fusion(bf16[1024,256]{1,0:T(8,128)(2,1)} %param.8, bf16[1024,1024]{1,0:T(8,128)(2,1)S(1)} %copy-done, bf16[1024,1024]{1,0:T(8,128)(2,1)} %param.7), kind=kOutput, calls=%fused_computation.17 | convolution fusion | flops 2694315008 | bytes 5771264 | tf_op jit(solution)/shard_map/dot_general | solution.py:164
  13.8 3.8 %sort.15 = (s32[1024]{0:T(1024)S(1)}, s32[1024]{0:T(1024)S(1)}) sort(s32[1024]{0:T(1024)S(1)} %copy-done.3, s32[1024]{0:T(1024)S(1)} %iota.19), dimensions={0}, to_apply=%region_0.0 | sort | flops 10240 | bytes 16384 | tf_op jit(solution)/shard_map/sort | solution.py:158
  17.5 1.7 fusion.12.own_emb
  19.2 0.0 all-gather.3.cloned.1.call-update
  19.2 69.7 %all-gather = s32[32768]{0:T(1024)S(1)} all-gather(s32[1024]{0:T(1024)S(1)} %get-tuple-element.4), channel_id=2, replica_groups=mesh['wide'=8,'rep'=4] {'wide','rep'}, dimensions={0}, use_global_device_ids=true | all-gather | bytes 135168 | tf_op jit(solution)/shard_map/all_gather | solution.py:159
  89.0 0.1 convert_reduce_fusion.3
  89.2 0.7 fusion.21
  105.1 0.1 constant_dynamic-slice_fusion
  105.2 0.1 constant_dynamic-slice_fusion.2
  105.3 0.1 constant_dynamic-slice_fusion.4
  105.3 0.1 constant_dynamic-slice_fusion.6
  105.5 16.7 %gather_fusion = bf16[3072,256]{1,0:T(8,128)(2,1)} fusion(bf16[16384,256]{1,0:T(8,128)(2,1)} %cent.1, s32[3072]{0:T(1024)S(1)} %broadcast_clamp_fusion), kind=kCustom, calls=%fused_computation | custom fusion | bytes 3158016 | tf_op jit(solution)/shard_map/gather | solution.py:178
  122.2 5.9 %all-to-all-start = ((bf16[8,384,256]{2,1,0:T(8,128)(2,1)}), bf16[8,384,256]{2,1,0:T(8,128)(2,1)}, u32[]{:S(2)}, u32[]{:S(2)}) async-start(bf16[8,384,256]{2,1,0:T(8,128)(2,1)} %bitcast.30), calls=%async_computation | async-start | bytes 3145728 | tf_op jit(solution)/shard_map/all_to_all | solution.py:179
  128.1 0.1 slice.55
  128.2 0.1 slice.54
  128.3 0.1 pad_add_fusion.1
  128.4 0.3 convert_reduce_fusion
  128.7 0.1 reshape.83.first
  128.8 0.1 reshape.84.last
  128.9 0.2 copy.9.own_ids
  129.1 0.1 pad_add_fusion.scalars
  129.2 0.2 convert_reduce_fusion.2
  129.4 0.1 select_reduce_fusion
  129.5 18.2 %all-to-all-done = bf16[8,384,256]{2,1,0:T(8,128)(2,1)} async-done(((bf16[8,384,256]{2,1,0:T(8,128)(2,1)}), bf16[8,384,256]{2,1,0:T(8,128)(2,1)}, u32[]{:S(2)}, u32[]{:S(2)}) %all-to-all-start) | async-done | bytes 1572896 | tf_op jit(solution)/shard_map/all_to_all | solution.py:179
  147.7 6.2 %gather_fusion.1 = bf16[1024,256]{1,0:T(8,128)(2,1)} fusion(bf16[3072,256]{1,0:T(8,128)(2,1)} %bitcast.14, s32[1024]{0:T(1024)S(1)} %fusion.15), kind=kCustom, calls=%fused_computation.1 | custom fusion | bytes 1052672 | tf_op jit(solution)/shard_map/gather | solution.py:189
  153.9 0.0 copy-done.1
  154.0 1.0 copy-done.2
  155.0 75.4 %shard_map.68 = (bf16[4096,256]{1,0:T(8,128)(2,1)}, bf16[1024,256]{1,0:T(8,128)(2,1)}) custom-call(s32[2]{0:T(128)S(1)} %pad_add_fusion.scalars, s32[160]{0:T(256)S(1)} %reshape.83.first, s32[160]{0:T(256)S(1)} %reshape.84.last, bf16[32768,256]{1,0:T(8,128)(2,1)} %all-gather.3.cloned.1.call-done.emb, s32[264,128]{1,0:T(8,128)S(1)} %concatenate.11.ids, ...), custom_call_target="tpu_custom_call" | custom-call | flops 30000001024 | bytes 40000000 | tf_op jit(solution)/shard_map/pallas_call | solution.py:204
  (21 shorter events, 0.3 us)
Async XLA Ops:
  7.2 1.6 copy-start
  7.2 6.6 %copy-start.3 = (s32[1024]{0:T(1024)S(1)}, s32[1024]{0:T(1024)}, u32[]{:S(2)}) copy-start(s32[1024]{0:T(1024)} %param.6) | copy-start | bytes 12292
  7.2 146.8 %all-gather.3.cloned.1.call-start = ((), (), s32[]{:S(2)}) async-start(), calls=%async_computation.1 | async-start | bytes 17301504 | tf_op jit(solution)/shard_map/all_gather | solution.py:168
  122.2 31.8 %copy-start.1 = (bf16[1024,256]{1,0:T(8,128)(2,1)S(1)}, bf16[1024,256]{1,0:T(8,128)(2,1)}, u32[]{:S(2)}) copy-start(bf16[1024,256]{1,0:T(8,128)(2,1)} %fusion.12.own_emb) | copy-start | bytes 1572868
  122.2 25.5 %all-to-all-start = ((bf16[8,384,256]{2,1,0:T(8,128)(2,1)}), bf16[8,384,256]{2,1,0:T(8,128)(2,1)}, u32[]{:S(2)}, u32[]{:S(2)}) async-start(bf16[8,384,256]{2,1,0:T(8,128)(2,1)} %bitcast.30), calls=%async_computation | async-start | bytes 3145728 | tf_op jit(solution)/shard_map/all_to_all | solution.py:179
  153.9 1.0 copy-start.2
Sparse Core Ops, SparseCore 0:
  19.4 117.2 all-gather.2

commit v2 on v1

--- a/solution.py
+++ b/solution.py
@@ -10,6 +10,7 @@
 CHUNK = 128
 GROUP = 8
 EPS = 1e-06
+WIDE = ("chip", "core")
 
 
 def normalised(values):
@@ -19,7 +20,7 @@
 def sums_kernel(
     scalars, first, last, emb, ids, cent, own_ids, own_cent, own_emb, order,
     out_table, out_res, chunks, slots, acc, cent_buf, tile_res, sems, cent_sem,
-    *, blocks, per_block, tile, row_block,
+    *, blocks, per_block, stride, tile, row_block, resident,
 ):
     n_chunks = blocks * per_block
     share = out_table.shape[0]
@@ -30,6 +31,22 @@
         cent.at[pl.ds(pl.multiple_of(scalars[1], 16), share)], cent_buf, cent_sem
     )
     cent_copy.start()
+
+    def row_of(n):
+        return pl.multiple_of(lax.div(n, per_block) * stride + lax.rem(n, per_block) * CHUNK, 16)
+
+    def whole_copies():
+        rows = emb.shape[0] // GROUP
+        return [
+            pltpu.make_async_copy(
+                emb.at[pl.ds(j * rows, rows)], slots.at[pl.ds(j * rows, rows)], sems.at[0, j]
+            )
+            for j in range(GROUP)
+        ]
+
+    if resident:
+        for copy in whole_copies():
+            copy.start()
 
     def build(job):
         def block(k, count):
@@ -55,14 +72,27 @@
             at = jnp.minimum(chunks[group * GROUP + j], n_chunks - 1)
             made.append(
                 pltpu.make_async_copy(
-                    emb.at[pl.ds(pl.multiple_of(at * CHUNK, CHUNK), CHUNK)],
+                    emb.at[pl.ds(row_of(at), CHUNK)],
                     slots.at[slot, pl.ds(j * CHUNK, CHUNK)],
                     sems.at[slot, j],
                 )
             )
         return made
 
-    def run(groups, step):
+    def id_row_of(group):
+        row = [ids[pl.ds(chunks[group * GROUP + j], 1), :] for j in range(GROUP)]
+        return jnp.concatenate(row, axis=1)
+
+    def run_resident(groups, step):
+        def body(group, carry):
+            at = [jnp.minimum(chunks[group * GROUP + j], n_chunks - 1) for j in range(GROUP)]
+            rows = jnp.concatenate([slots[pl.ds(row_of(n), CHUNK), :] for n in at], axis=0)
+            step(id_row_of(group), rows)
+            return carry
+
+        lax.fori_loop(0, groups, body, 0)
+
+    def run_streamed(groups, step):
         @pl.when(groups > 0)
         def _():
             for copy in copies(0, 0):
@@ -78,22 +108,26 @@
 
             for copy in copies(group, slot):
                 copy.wait()
-            row = [ids[pl.ds(chunks[group * GROUP + j], 1), :] for j in range(GROUP)]
-            step(jnp.concatenate(row, axis=1), slot)
+            step(id_row_of(group), slots[slot])
             return carry
 
         lax.fori_loop(0, groups, body, 0)
+
+    run = run_resident if resident else run_streamed
 
     acc[...] = jnp.zeros_like(acc)
     groups = build(0)
-
-    def table_step(id_row, slot):
+    if resident:
+        for copy in whole_copies():
+            copy.wait()
+
+    def table_step(id_row, values):
         def rows(m, carry):
             at = pl.multiple_of(m * row_block, row_block)
             wanted = scalars[0] + at + lax.broadcasted_iota(jnp.int32, (row_block, wide), 0)
             pick = (wanted == id_row).astype(jnp.float32).astype(jnp.bfloat16)
             acc[pl.ds(at, row_block), :] += jnp.dot(
-                pick, slots[slot], preferred_element_type=jnp.float32
+                pick, values, preferred_element_type=jnp.float32
             )
             return carry
 
@@ -116,9 +150,9 @@
         part[...] = jnp.zeros((tile, acc.shape[1]), jnp.float32)
         groups = build(i + 1)
 
-        def tile_step(id_row, slot):
+        def tile_step(id_row, values):
             pick = (own_ids[at, :] == id_row).astype(jnp.float32).astype(jnp.bfloat16)
-            part[...] += jnp.dot(pick, slots[slot], preferred_element_type=jnp.float32)
+            part[...] += jnp.dot(pick, values, preferred_element_type=jnp.float32)
 
         run(groups, tile_step)
         fresh = normalised(own_cent[at, :].astype(jnp.float32) + part[...]).astype(jnp.bfloat16)
@@ -143,7 +177,7 @@
 
 def body(passages, cluster_ids, w_first, w_second, centroids):
     tok = passages.shape[0]
-    owners = lax.axis_size("wide")
+    owners = lax.axis_size(WIDE)
     reps = lax.axis_size("rep")
     blocks = owners * reps
     cent_rows, emb_width = centroids.shape
@@ -152,11 +186,10 @@
     per_block = tok // CHUNK
     tile = min(256, tok)
     tiles = tok // tile
-    wide_at = lax.axis_index("wide")
+    wide_at = lax.axis_index(WIDE)
     rep_at = lax.axis_index("rep")
 
     sorted_ids, order = lax.sort((cluster_ids, lax.iota(jnp.int32, tok)), num_keys=1)
-    all_ids = lax.all_gather(sorted_ids, ("wide", "rep"), axis=0, tiled=False)
 
     hidden = jax.nn.gelu(
         jnp.dot(passages, w_first, preferred_element_type=jnp.float32), approximate=True
@@ -165,25 +198,37 @@
     embedded = normalised(projected).astype(jnp.bfloat16)
     to_sorted = (order[:, None] == jnp.arange(tok, dtype=jnp.int32)[None, :]).astype(jnp.bfloat16)
     own_emb = jnp.dot(to_sorted, embedded, preferred_element_type=jnp.float32).astype(jnp.bfloat16)
-    all_emb = lax.all_gather(own_emb, ("wide", "rep"), axis=0, tiled=True)
-
-    mine = lax.dynamic_index_in_dim(all_ids.reshape(owners, reps, tok), rep_at, 1, keepdims=False)
+    id_bytes = jnp.stack([sorted_ids // 65536, sorted_ids // 256 % 256, sorted_ids % 256])
+    id_part = id_bytes.astype(jnp.bfloat16).reshape(3 * tok // emb_width, emb_width)
+    stride = tok + -(-id_part.shape[0] // 16) * 16
+    outgoing = jnp.concatenate(
+        [own_emb, jnp.pad(id_part, ((0, stride - tok - id_part.shape[0]), (0, 0)))]
+    )
+    same_core = lax.all_gather(outgoing, ("chip", "rep"), axis=0, tiled=True)
+    all_emb = lax.all_gather(same_core, "core", axis=0, tiled=True)
+    id_parts = all_emb.reshape(blocks, stride, emb_width)[:, tok : tok + id_part.shape[0]]
+    id_parts = id_parts.astype(jnp.int32).reshape(blocks, 3, tok)
+    all_ids = id_parts[:, 0] * 65536 + id_parts[:, 1] * 256 + id_parts[:, 2]
+
     owner_base = wide_at * cent_rows
-    begin = jnp.sum((mine < owner_base).astype(jnp.int32), axis=1)
-    padded = jnp.pad(mine, ((0, 0), (0, capacity)))
-    asked = jnp.stack(
-        [lax.dynamic_slice(padded[k], (begin[k],), (capacity,)) for k in range(owners)]
-    )
-    local = jnp.clip(asked - owner_base, 0, cent_rows - 1).reshape(owners * capacity)
-    picked = centroids[local]
-    returned = lax.all_to_all(picked, "wide", split_axis=0, concat_axis=0, tiled=True)
-    owner_of = sorted_ids // cent_rows
     starts = jnp.sum(
         (sorted_ids[None, :] < jnp.arange(owners, dtype=jnp.int32)[:, None] * cent_rows).astype(
             jnp.int32
         ),
         axis=1,
     )
+    ask_at = (starts[:, None] + jnp.arange(capacity, dtype=jnp.int32)[None, :]).reshape(-1)
+    ask = jnp.sum(
+        jnp.where(
+            ask_at[:, None] == jnp.arange(tok, dtype=jnp.int32)[None, :], sorted_ids[None, :], 0
+        ),
+        axis=1,
+    )
+    asked = lax.all_to_all(ask, WIDE, split_axis=0, concat_axis=0, tiled=True)
+    local = jnp.clip(asked - owner_base, 0, cent_rows - 1)
+    picked = centroids[local]
+    returned = lax.all_to_all(picked, WIDE, split_axis=0, concat_axis=0, tiled=True)
+    owner_of = sorted_ids // cent_rows
     member = (owner_of[:, None] == jnp.arange(owners, dtype=jnp.int32)[None, :]).astype(jnp.int32)
     place = owner_of * capacity + lax.iota(jnp.int32, tok) - jnp.sum(member * starts[None, :], axis=1)
     own_cent = returned[place]
@@ -198,12 +243,15 @@
         [all_ids.reshape(blocks * per_block, CHUNK), jnp.full((8, CHUNK), -1, jnp.int32)]
     )
 
+    resident = all_emb.size * 2 <= 24 * 1024 * 1024 and all_emb.shape[0] % (16 * GROUP) == 0
+    held = all_emb.shape if resident else (2, GROUP * CHUNK, emb_width)
     smem = pl.BlockSpec(memory_space=pltpu.SMEM)
     vmem = pl.BlockSpec(memory_space=pltpu.VMEM)
     hbm = pl.BlockSpec(memory_space=pl.ANY)
     return pl.pallas_call(
         functools.partial(
-            sums_kernel, blocks=blocks, per_block=per_block, tile=tile, row_block=min(512, share)
+            sums_kernel, blocks=blocks, per_block=per_block, stride=stride, tile=tile,
+            row_block=min(512, share), resident=resident,
         ),
         out_shape=(
             jax.ShapeDtypeStruct((share, emb_width), jnp.bfloat16),
@@ -213,7 +261,7 @@
         out_specs=(vmem, vmem),
         scratch_shapes=[
             pltpu.SMEM((blocks * per_block + GROUP,), jnp.int32),
-            pltpu.VMEM((2, GROUP * CHUNK, emb_width), jnp.bfloat16),
+            pltpu.VMEM(held, jnp.bfloat16),
             pltpu.VMEM((share, emb_width), jnp.float32),
             pltpu.VMEM((share, emb_width), jnp.bfloat16),
             pltpu.VMEM((tok, emb_width), jnp.bfloat16),
@@ -231,10 +279,13 @@
 
 
 def solution(mesh):
+    wide, rep = mesh.devices.shape
+    mesh = jax.sharding.Mesh(mesh.devices.reshape(wide // 2, 2, rep), ("chip", "core", "rep"))
+    every = ("chip", "core", "rep")
     return jax.shard_map(
         body,
         mesh=mesh,
-        in_specs=(P(("wide", "rep"), None), P(("wide", "rep")), P(), P(), P("wide", None)),
-        out_specs=(P(("wide", "rep"), None), P(("wide", "rep"), None)),
+        in_specs=(P(every, None), P(every), P(), P(), P(WIDE, None)),
+        out_specs=(P(every, None), P(every, None)),
         check_vma=False,
     )

time: 240 us -> 273 us (1.14)
  the two profiles are of different devices: /device:TPU:4 before, /device:TPU:26 now
where the time goes in v2:
time: 273 us; the launch traced here: 271 us
  waiting for transfers between devices  135 us (49%)
  Pallas kernels  62.2 us (23%)
  local copies, waits for them, and re-layouts  29.1 us (11%)
  between operations  14.2 us (5%)
  other arithmetic  13 us (5%)
  starting transfers between devices  9.37 us (3%)
  matrix products  8.02 us (3%)
    all_gather x1, waiting for transfers between devices, body(): same_core = lax.all_gather(outgoing, ('chip', 'rep'), axis=0, tiled=True)  113 us
    pallas_call x1, Pallas kernels, body(): pl.pallas_call(functools.partial(sums_kernel, blocks=blocks, per_block=pe...  62.2 us
    gather x1, local copies, waits for them, and re-layouts, body(): picked = centroids[local]  19.2 us
    all_to_all x1, waiting for transfers between devices, body(): lax.all_to_all(picked, WIDE, split_axis=0, concat_axis=0, tiled=True)  19 us
    gather x1, local copies, waits for them, and re-layouts, body(): own_cent = returned[place]  6.17 us
    dot_general x1, matrix products, body(): projected = jnp.dot(hidden, w_second, preferred_element_type=jnp.float32)  5.94 us
    all_to_all x1, starting transfers between devices, body(): lax.all_to_all(picked, WIDE, split_axis=0, concat_axis=0, tiled=True)  5.46 us
  transfers between devices with their start and end apart: 4, of which 3 were waited for; matrix products, arithmetic and copies ran while one was open for 11% of the time, Pallas kernels for 0%

profile of v2, /device:TPU:26, one launch (start us, length us, event | category | flops | bytes accessed | tf_op | source)
XLA Modules:
  0.0 271.3 jit_solution(8546738480381012590)
XLA Ops:
  7.2 0.0 all-gather.3.cloned.1.call-start
  7.2 4.6 %sort.15 = (s32[1024]{0:T(1024)S(1)}, s32[1024]{0:T(1024)S(1)}) sort(s32[1024]{0:T(1024)} %param.6, s32[1024]{0:T(1024)S(1)} %iota.25), dimensions={0}, to_apply=%region_0.0 | sort | flops 10240 | bytes 16384 | tf_op jit(solution)/shard_map/sort | solution.py:192
  11.9 0.2 convert_reduce_fusion.2
  12.0 0.1 select_reduce_fusion.1
  12.3 5.9 %multiply_reduce_fusion = (f32[1024]{0:T(1024)S(1)}, f32[1024,256]{0,1:T(8,128)}) fusion(bf16[1024,256]{1,0:T(8,128)(2,1)} %param.8, bf16[1024,1024]{1,0:T(8,128)(2,1)S(1)} %copy-done, bf16[1024,1024]{1,0:T(8,128)(2,1)} %param.7), kind=kOutput, calls=%fused_computation.21 | convolution fusion | flops 2694315008 | bytes 5771264 | tf_op jit(solution)/shard_map/dot_general | solution.py:197
  18.2 2.1 fusion.12.own_emb
  20.3 0.8 fusion.14
  21.1 0.0 all-gather.3.cloned.1.call-update
  21.2 0.0 all-gather.5.cloned.1.call-start
  21.2 113.1 %all-gather.3.cloned.1.call-done = bf16[16640,256]{1,0:T(8,128)(2,1)} async-done(((bf16[1040,256]{1,0:T(8,128)(2,1)}), bf16[16640,256]{1,0:T(8,128)(2,1)}) %all-gather.3.cloned.1.call-update) | async-done | bytes 8519696 | tf_op jit(solution)/shard_map/all_gather | solution.py:207
  134.3 0.1 iota_add_fusion
  134.4 2.9 %select_reduce_fusion = s32[3072]{0:T(1024)} fusion(s32[1024]{0:T(1024)S(1)} %get-tuple-element.5, s32[3072]{0:T(1024)S(1)} %add.133), kind=kLoop, calls=%fused_computation.2 | loop fusion | flops 9434112 | bytes 28672 | tf_op jit(solution)/shard_map/reduce_sum | solution.py:221
  137.3 3.8 %all-to-all-start = ((s32[8,384,1]{1,2,0:T(1,128)}), s32[8,384,1]{1,2,0:T(1,128)S(1)}, u32[]{:S(2)}, u32[]{:S(2)}) async-start(s32[8,384,1]{1,2,0:T(1,128)} %bitcast.5), calls=%async_computation | async-start | bytes 24576 | tf_op jit(solution)/shard_map/all_to_all | solution.py:227
  141.1 3.3 %all-to-all-done = s32[8,384,1]{1,2,0:T(1,128)S(1)} async-done(((s32[8,384,1]{1,2,0:T(1,128)}), s32[8,384,1]{1,2,0:T(1,128)S(1)}, u32[]{:S(2)}, u32[]{:S(2)}) %all-to-all-start) | async-done | bytes 12320 | tf_op jit(solution)/shard_map/all_to_all | solution.py:227
  144.4 19.2 %gather_fusion = bf16[3072,256]{1,0:T(8,128)(2,1)} fusion(bf16[16384,256]{1,0:T(8,128)(2,1)} %cent.1, s32[3072]{0:T(1024)S(1)} %broadcast_clamp_fusion), kind=kCustom, calls=%fused_computation | custom fusion | bytes 3158016 | tf_op jit(solution)/shard_map/gather | solution.py:229
  163.6 5.5 %all-to-all-start.1 = ((bf16[8,384,256]{2,1,0:T(8,128)(2,1)}), bf16[8,384,256]{2,1,0:T(8,128)(2,1)}, u32[]{:S(2)}, u32[]{:S(2)}) async-start(bf16[8,384,256]{2,1,0:T(8,128)(2,1)} %bitcast.18), calls=%async_computation.1 | async-start | bytes 3145728 | tf_op jit(solution)/shard_map/all_to_all | solution.py:230
  169.1 0.1 slice.23
  169.2 0.1 slice.22
  169.3 0.2 copy.14.own_ids
  169.5 0.1 pad_add_fusion.1
  169.6 0.1 pad_add_fusion.scalars
  169.7 0.1 pad_add_fusion.2
  169.7 19.0 %all-to-all-done.1 = bf16[8,384,256]{2,1,0:T(8,128)(2,1)} async-done(((bf16[8,384,256]{2,1,0:T(8,128)(2,1)}), bf16[8,384,256]{2,1,0:T(8,128)(2,1)}, u32[]{:S(2)}, u32[]{:S(2)}) %all-to-all-start.1) | async-done | bytes 1572896 | tf_op jit(solution)/shard_map/all_to_all | solution.py:230
  188.7 6.2 %gather_fusion.1 = bf16[1024,256]{1,0:T(8,128)(2,1)} fusion(bf16[3072,256]{1,0:T(8,128)(2,1)} %bitcast.9, s32[1024]{0:T(1024)S(1)} %get-tuple-element.8), kind=kCustom, calls=%fused_computation.1 | custom fusion | bytes 1052672 | tf_op jit(solution)/shard_map/gather | solution.py:234
  194.9 1.8 slice_convert_fusion
  196.7 2.0 reshape.125
  198.8 1.8 slice_add_fusion
  200.6 0.3 convert_reduce_fusion
  201.0 0.1 reshape.122.first
  201.1 0.1 reshape.123.last
  201.2 1.0 copy-done.1
  202.2 62.2 %shard_map.68 = (bf16[4096,256]{1,0:T(8,128)(2,1)}, bf16[1024,256]{1,0:T(8,128)(2,1)}) custom-call(s32[2]{0:T(128)S(1)} %pad_add_fusion.scalars, s32[160]{0:T(256)S(1)} %reshape.122.first, s32[160]{0:T(256)S(1)} %reshape.123.last, bf16[33280,256]{1,0:T(8,128)(2,1)} %all-gather.5.cloned.1.call-done.emb, s32[264,128]{1,0:T(8,128)S(1)} %concatenate.15.ids, ...), custom_call_target="tpu_custom_call" | custom-call | flops 30000001024 | bytes 40000000 | tf_op jit(solution)/shard_map/pallas_call | solution.py:251
  (22 shorter events, 0.2 us)
Async XLA Ops:
  7.2 5.1 %copy-start = (bf16[1024,1024]{1,0:T(8,128)(2,1)S(1)}, bf16[1024,1024]{1,0:T(8,128)(2,1)}, u32[]{:S(2)}) copy-start(bf16[1024,1024]{1,0:T(8,128)(2,1)} %param.5) | copy-start | bytes 6291460
  7.2 127.1 %all-gather.3.cloned.1.call-start = ((), (), s32[]{:S(2)}) async-start(), calls=%async_computation.2 | async-start | bytes 9052160 | tf_op jit(solution)/shard_map/all_gather | solution.py:207
  21.2 173.8 %all-gather.5.cloned.1.call-start = ((), (), s32[]{:S(2)}) async-start(), calls=%async_computation.3 | async-start | bytes 25559040 | tf_op jit(solution)/shard_map/all_gather | solution.py:208
  137.3 7.1 %all-to-all-start = ((s32[8,384,1]{1,2,0:T(1,128)}), s32[8,384,1]{1,2,0:T(1,128)S(1)}, u32[]{:S(2)}, u32[]{:S(2)}) async-start(s32[8,384,1]{1,2,0:T(1,128)} %bitcast.5), calls=%async_computation | async-start | bytes 24576 | tf_op jit(solution)/shard_map/all_to_all | solution.py:227
  163.6 25.1 %all-to-all-start.1 = ((bf16[8,384,256]{2,1,0:T(8,128)(2,1)}), bf16[8,384,256]{2,1,0:T(8,128)(2,1)}, u32[]{:S(2)}, u32[]{:S(2)}) async-start(bf16[8,384,256]{2,1,0:T(8,128)(2,1)} %bitcast.18), calls=%async_computation.1 | async-start | bytes 3145728 | tf_op jit(solution)/shard_map/all_to_all | solution.py:230
  201.2 1.0 copy-start.1
Sparse Core Ops, SparseCore 0:
  21.3 112.9 all-gather.2
  135.9 32.2 all-gather.4

commit v3 on v2

--- a/solution.py
+++ b/solution.py
@@ -7,10 +7,10 @@
 from jax.experimental.pallas import tpu as pltpu
 from jax.sharding import PartitionSpec as P
 
-CHUNK = 128
-GROUP = 8
+CHUNK = 64
+GROUP = 16
 EPS = 1e-06
-WIDE = ("chip", "core")
+WIDE = "wide"
 
 
 def normalised(values):
@@ -36,12 +36,12 @@
         return pl.multiple_of(lax.div(n, per_block) * stride + lax.rem(n, per_block) * CHUNK, 16)
 
     def whole_copies():
-        rows = emb.shape[0] // GROUP
+        rows = emb.shape[0] // 8
         return [
             pltpu.make_async_copy(
                 emb.at[pl.ds(j * rows, rows)], slots.at[pl.ds(j * rows, rows)], sems.at[0, j]
             )
-            for j in range(GROUP)
+            for j in range(8)
         ]
 
     if resident:
@@ -204,8 +204,7 @@
     outgoing = jnp.concatenate(
         [own_emb, jnp.pad(id_part, ((0, stride - tok - id_part.shape[0]), (0, 0)))]
     )
-    same_core = lax.all_gather(outgoing, ("chip", "rep"), axis=0, tiled=True)
-    all_emb = lax.all_gather(same_core, "core", axis=0, tiled=True)
+    all_emb = lax.all_gather(outgoing, ("wide", "rep"), axis=0, tiled=True)
     id_parts = all_emb.reshape(blocks, stride, emb_width)[:, tok : tok + id_part.shape[0]]
     id_parts = id_parts.astype(jnp.int32).reshape(blocks, 3, tok)
     all_ids = id_parts[:, 0] * 65536 + id_parts[:, 1] * 256 + id_parts[:, 2]
@@ -243,7 +242,7 @@
         [all_ids.reshape(blocks * per_block, CHUNK), jnp.full((8, CHUNK), -1, jnp.int32)]
     )
 
-    resident = all_emb.size * 2 <= 24 * 1024 * 1024 and all_emb.shape[0] % (16 * GROUP) == 0
+    resident = all_emb.size * 2 <= 24 * 1024 * 1024 and all_emb.shape[0] % 128 == 0
     held = all_emb.shape if resident else (2, GROUP * CHUNK, emb_width)
     smem = pl.BlockSpec(memory_space=pltpu.SMEM)
     vmem = pl.BlockSpec(memory_space=pltpu.VMEM)
@@ -279,13 +278,10 @@
 
 
 def solution(mesh):
-    wide, rep = mesh.devices.shape
-    mesh = jax.sharding.Mesh(mesh.devices.reshape(wide // 2, 2, rep), ("chip", "core", "rep"))
-    every = ("chip", "core", "rep")
     return jax.shard_map(
         body,
         mesh=mesh,
-        in_specs=(P(every, None), P(every), P(), P(), P(WIDE, None)),
-        out_specs=(P(every, None), P(every, None)),
+        in_specs=(P(("wide", "rep"), None), P(("wide", "rep")), P(), P(), P("wide", None)),
+        out_specs=(P(("wide", "rep"), None), P(("wide", "rep"), None)),
         check_vma=False,
     )

time: 273 us -> 220 us (0.81)
  the two profiles are of different devices: /device:TPU:26 before, /device:TPU:2 now
where the time goes in v3:
time: 220 us
  waiting for transfers between devices  91.7 us (42%)
  Pallas kernels  54.7 us (25%)
  local copies, waits for them, and re-layouts  26.9 us (12%)
  other arithmetic  15 us (7%)
  between operations  14.2 us (6%)
  starting transfers between devices  9.84 us (4%)
  matrix products  8.03 us (4%)
    all_gather x1, waiting for transfers between devices, body(): all_emb = lax.all_gather(outgoing, ('wide', 'rep'), axis=0, tiled=True)  59.3 us
    pallas_call x1, Pallas kernels, body(): pl.pallas_call(functools.partial(sums_kernel, blocks=blocks, per_block=pe...  54.7 us
    all_to_all x1, waiting for transfers between devices, body(): lax.all_to_all(picked, WIDE, split_axis=0, concat_axis=0, tiled=True)  29.2 us
    gather x1, local copies, waits for them, and re-layouts, body(): picked = centroids[local]  16.8 us
    gather x1, local copies, waits for them, and re-layouts, body(): own_cent = returned[place]  6.21 us
    dot_general x1, matrix products, body(): projected = jnp.dot(hidden, w_second, preferred_element_type=jnp.float32)  5.95 us
    all_to_all x1, starting transfers between devices, body(): lax.all_to_all(picked, WIDE, split_axis=0, concat_axis=0, tiled=True)  5.55 us
    sort x1, other arithmetic, body(): lax.sort((cluster_ids, lax.iota(jnp.int32, tok)), num_keys=1)  4.58 us
  transfers between devices with their start and end apart: 3, of which 3 were waited for; matrix products, arithmetic and copies ran while one was open for 13% of the time, Pallas kernels for 0%

profile of v3, /device:TPU:2, one launch (start us, length us, event | category | flops | bytes accessed | tf_op | source)
XLA Modules:
  0.0 220.4 jit_solution(7390428802495557492)
XLA Ops:
  7.2 0.0 all-gather.2.cloned.1.call-start
  7.2 4.6 %sort.15 = (s32[1024]{0:T(1024)S(1)}, s32[1024]{0:T(1024)S(1)}) sort(s32[1024]{0:T(1024)} %param.6, s32[1024]{0:T(1024)S(1)} %iota.25), dimensions={0}, to_apply=%region_0.0 | sort | flops 10240 | bytes 16384 | tf_op jit(solution)/shard_map/sort | solution.py:192
  11.9 0.2 convert_reduce_fusion.2
  12.0 0.1 select_reduce_fusion.1
  12.3 5.9 %multiply_reduce_fusion = (f32[1024]{0:T(1024)S(1)}, f32[1024,256]{0,1:T(8,128)}) fusion(bf16[1024,256]{1,0:T(8,128)(2,1)} %param.8, bf16[1024,1024]{1,0:T(8,128)(2,1)S(1)} %copy-done, bf16[1024,1024]{1,0:T(8,128)(2,1)} %param.7), kind=kOutput, calls=%fused_computation.21 | convolution fusion | flops 2694315008 | bytes 5771264 | tf_op jit(solution)/shard_map/dot_general | solution.py:197
  18.2 2.1 fusion.12.own_emb
  20.3 0.8 fusion.14
  21.1 0.0 all-gather.2.cloned.1.call-update
  21.2 0.1 iota_add_fusion
  21.2 2.9 %select_reduce_fusion = s32[3072]{0:T(1024)} fusion(s32[1024]{0:T(1024)S(1)} %get-tuple-element.5, s32[3072]{0:T(1024)S(1)} %add.129), kind=kLoop, calls=%fused_computation.2 | loop fusion | flops 9434112 | bytes 28672 | tf_op jit(solution)/shard_map/reduce_sum | solution.py:220
  24.1 4.3 %all-to-all-start = ((s32[8,384,1]{1,2,0:T(1,128)}), s32[8,384,1]{1,2,0:T(1,128)S(1)}, u32[]{:S(2)}, u32[]{:S(2)}) async-start(s32[8,384,1]{1,2,0:T(1,128)} %bitcast.4), calls=%async_computation | async-start | bytes 24576 | tf_op jit(solution)/shard_map/all_to_all | solution.py:226
  28.4 3.3 %all-to-all-done = s32[8,384,1]{1,2,0:T(1,128)S(1)} async-done(((s32[8,384,1]{1,2,0:T(1,128)}), s32[8,384,1]{1,2,0:T(1,128)S(1)}, u32[]{:S(2)}, u32[]{:S(2)}) %all-to-all-start) | async-done | bytes 12320 | tf_op jit(solution)/shard_map/all_to_all | solution.py:226
  31.7 16.8 %gather_fusion = bf16[3072,256]{1,0:T(8,128)(2,1)} fusion(bf16[16384,256]{1,0:T(8,128)(2,1)} %cent.1, s32[3072]{0:T(1024)S(1)} %broadcast_clamp_fusion), kind=kCustom, calls=%fused_computation | custom fusion | bytes 3158016 | tf_op jit(solution)/shard_map/gather | solution.py:228
  48.5 5.6 %all-to-all-start.1 = ((bf16[8,384,256]{2,1,0:T(8,128)(2,1)}), bf16[8,384,256]{2,1,0:T(8,128)(2,1)}, u32[]{:S(2)}, u32[]{:S(2)}) async-start(bf16[8,384,256]{2,1,0:T(8,128)(2,1)} %bitcast.17), calls=%async_computation.1 | async-start | bytes 3145728 | tf_op jit(solution)/shard_map/all_to_all | solution.py:229
  54.1 0.1 slice.23
  54.2 0.1 slice.22
  54.3 0.2 copy.14.own_ids
  54.5 0.7 pad_add_fusion.1
  55.2 0.1 pad_add_fusion.scalars
  55.2 0.6 pad_add_fusion.2
  55.8 29.2 %all-to-all-done.1 = bf16[8,384,256]{2,1,0:T(8,128)(2,1)} async-done(((bf16[8,384,256]{2,1,0:T(8,128)(2,1)}), bf16[8,384,256]{2,1,0:T(8,128)(2,1)}, u32[]{:S(2)}, u32[]{:S(2)}) %all-to-all-start.1) | async-done | bytes 1572896 | tf_op jit(solution)/shard_map/all_to_all | solution.py:229
  85.0 6.2 %gather_fusion.1 = bf16[1024,256]{1,0:T(8,128)(2,1)} fusion(bf16[3072,256]{1,0:T(8,128)(2,1)} %bitcast.8, s32[1024]{0:T(1024)S(1)} %get-tuple-element.10), kind=kCustom, calls=%fused_computation.1 | custom fusion | bytes 1052672 | tf_op jit(solution)/shard_map/gather | solution.py:233
  91.2 59.3 %all-gather.2.cloned.1.call-done.emb = bf16[33280,256]{1,0:T(8,128)(2,1)} async-done(((bf16[1040,256]{1,0:T(8,128)(2,1)}), bf16[33280,256]{1,0:T(8,128)(2,1)}) %all-gather.2.cloned.1.call-update) | async-done | bytes 17039376 | tf_op jit(solution)/shard_map/all_gather | solution.py:207
  150.5 1.8 slice_convert_fusion
  152.3 2.0 reshape.125
  154.4 2.1 fusion.31
  156.5 1.0 convert_reduce_fusion
  157.5 0.1 reshape.122.first
  157.6 0.1 reshape.123.last
  157.6 0.1 add.125
  157.8 1.0 copy-done.1
  158.8 54.7 %shard_map.68 = (bf16[4096,256]{1,0:T(8,128)(2,1)}, bf16[1024,256]{1,0:T(8,128)(2,1)}) custom-call(s32[2]{0:T(128)S(1)} %pad_add_fusion.scalars, s32[160]{0:T(256)S(1)} %reshape.122.first, s32[160]{0:T(256)S(1)} %reshape.123.last, bf16[33280,256]{1,0:T(8,128)(2,1)} %all-gather.2.cloned.1.call-done.emb, s32[520,64]{1,0:T(8,128)S(1)} %concatenate.15.ids, ...), custom_call_target="tpu_custom_call" | custom-call | flops 30000001024 | bytes 40000000 | tf_op jit(solution)/shard_map/pallas_call | solution.py:250
  (20 shorter events, 0.2 us)
Async XLA Ops:
  7.2 5.1 %copy-start = (bf16[1024,1024]{1,0:T(8,128)(2,1)S(1)}, bf16[1024,1024]{1,0:T(8,128)(2,1)}, u32[]{:S(2)}) copy-start(bf16[1024,1024]{1,0:T(8,128)(2,1)} %param.5) | copy-start | bytes 6291460
  7.2 143.3 %all-gather.2.cloned.1.call-start = ((), (), s32[]{:S(2)}) async-start(), calls=%async_computation.2 | async-start | bytes 17571840 | tf_op jit(solution)/shard_map/all_gather | solution.py:207
  24.1 7.5 %all-to-all-start = ((s32[8,384,1]{1,2,0:T(1,128)}), s32[8,384,1]{1,2,0:T(1,128)S(1)}, u32[]{:S(2)}, u32[]{:S(2)}) async-start(s32[8,384,1]{1,2,0:T(1,128)} %bitcast.4), calls=%async_computation | async-start | bytes 24576 | tf_op jit(solution)/shard_map/all_to_all | solution.py:226
  48.5 36.5 %all-to-all-start.1 = ((bf16[8,384,256]{2,1,0:T(8,128)(2,1)}), bf16[8,384,256]{2,1,0:T(8,128)(2,1)}, u32[]{:S(2)}, u32[]{:S(2)}) async-start(bf16[8,384,256]{2,1,0:T(8,128)(2,1)} %bitcast.17), calls=%async_computation.1 | async-start | bytes 3145728 | tf_op jit(solution)/shard_map/all_to_all | solution.py:229
  157.8 1.0 copy-start.1
Sparse Core Ops, SparseCore 0:
  21.3 129.1 all-gather.1
